TPU v7x, 512 devices: a whole 4x8x8 slice. The times are simulated.
512 devices in a mesh: replica: 32 (over y, z_hi), tensor: 16 (over x, z_lo, core).
Axes of the slice: x: 4, y: 8, z: 8 (z_hi: 4, z_lo: 2; z = z_hi * 2 + z_lo), core: 2. Of those that a mesh axis runs over, the one named last changes fastest.
Arguments:
- activations: bfloat16 [32, 3072, 4096], P('replica', 'tensor'), may hold values from -6 to 6
- cotangent: bfloat16 [32, 3072, 512], P('replica', 'tensor'), may hold values from -6 to 6
- weight: float32 [32, 4096, 512], P('replica', 'tensor'), may hold values from -6 to 6
- first_moment: float32 [32, 4096, 512], P('replica', 'tensor'), may hold values from -3 to 3
- second_moment: float32 [32, 4096, 512], P('replica', 'tensor'), may hold values from 0.05 to 2
- anchor: float32 [4096, 512], P('tensor', 'replica'), may hold values from -6 to 6
- outer_momentum: float32 [4096, 512], P('tensor', 'replica'), may hold values from -2 to 2
- fragment_rows: int32 [4096], P('tensor'), may hold values 0 or 1
Outputs:
- weight_out: float32 [32, 4096, 512], P('replica', 'tensor')
- first_out: float32 [32, 4096, 512], P('replica', 'tensor')
- second_out: float32 [32, 4096, 512], P('replica', 'tensor')
- anchor_out: float32 [4096, 512], P('tensor', 'replica')
- momentum_out: float32 [4096, 512], P('tensor', 'replica')
- projected: bfloat16 [32, 3072, 512], P('replica', 'tensor')
All inputs are finite; a program needn't handle non-finite values. No bound on the sum of `fragment_rows` on one device may be relied on, other than what follows from the above.
Results may differ from a plain program's by a relative error of at most 0.011.
Values may be sent and summed in bfloat16 or wider, within the bound.
A program may use at most 64 MiB of HBM per device.

v0:
```python
import jax
import jax.numpy as jnp
from jax import lax
from jax.sharding import PartitionSpec as P

D = 4096
STEP = 20


FIRST_DECAY = 0.9
SECOND_DECAY = 0.95
ADAM_EPS = 1e-08
INNER_RATE = 0.02
WEIGHT_DECAY = 0.1
OUTER_RATE = 0.7
OUTER_MU = 0.9
MIX_SHARE = 0.5


def body(
    activations,
    cotangent,
    weight,
    first_moment,
    second_moment,
    anchor,
    outer_momentum,
    fragment_rows,
):
    inputs_here = activations[0]
    cotan_here = cotangent[0]
    weight_here = weight[0]
    multiplier = D ** (-0.5)
    weight_low = weight_here.astype(jnp.bfloat16)
    feature_cols = lax.all_to_all(inputs_here, "tensor", split_axis=1, concat_axis=0, tiled=True)
    token_rows = feature_cols
    projected = lax.psum_scatter(
        jnp.dot(token_rows, weight_low, preferred_element_type=jnp.float32) * multiplier,
        "tensor",
        scatter_dimension=0,
        tiled=True,
    ).astype(jnp.bfloat16)
    token_rows = feature_cols
    gradient = (
        lax.dot_general(
            token_rows,
            lax.all_gather(cotan_here, "tensor", axis=0, tiled=True),
            (((0,), (0,)), ((), ())),
            preferred_element_type=jnp.float32,
        )
        * multiplier
    )
    first_new = FIRST_DECAY * first_moment[0] + (1.0 - FIRST_DECAY) * gradient
    second_new = SECOND_DECAY * second_moment[0] + (1.0 - SECOND_DECAY) * gradient * gradient
    first_hat = first_new / (1.0 - FIRST_DECAY**STEP)
    second_hat = second_new / (1.0 - SECOND_DECAY**STEP)
    update = first_hat / (jnp.sqrt(second_hat) + ADAM_EPS) + WEIGHT_DECAY * weight_here
    inner = weight_here - INNER_RATE * update
    in_fragment = (fragment_rows == 1)[:, None]
    share_cols = anchor.shape[1]
    replica_count = lax.axis_size("replica")
    full_anchor, full_momentum = (
        lax.all_gather(anchor, "replica", axis=1, tiled=True),
        lax.all_gather(outer_momentum, "replica", axis=1, tiled=True),
    )
    summed_drift = lax.psum(full_anchor - weight_here, "replica")
    pseudo_grad = summed_drift / replica_count
    momentum_new = OUTER_MU * full_momentum + pseudo_grad
    anchor_new = full_anchor - OUTER_RATE * (pseudo_grad + OUTER_MU * momentum_new)
    anchor_full = jnp.where(in_fragment, anchor_new, full_anchor)
    momentum_full = jnp.where(in_fragment, momentum_new, full_momentum)
    offset_cols = lax.axis_index("replica") * share_cols
    anchor_out = lax.dynamic_slice_in_dim(anchor_full, offset_cols, share_cols, 1)
    momentum_out = lax.dynamic_slice_in_dim(momentum_full, offset_cols, share_cols, 1)
    merged = (1.0 - MIX_SHARE) * inner + MIX_SHARE * anchor_full
    weight_out = jnp.where(in_fragment, merged, inner)
    return (
        weight_out[None],
        first_new[None],
        second_new[None],
        anchor_out,
        momentum_out,
        projected[None],
    )


def solution(mesh):
    return jax.shard_map(
        body,
        mesh=mesh,
        in_specs=(
            P("replica", "tensor", None),
            P("replica", "tensor", None),
            P("replica", "tensor", None),
            P("replica", "tensor", None),
            P("replica", "tensor", None),
            P("tensor", "replica"),
            P("tensor", "replica"),
            P("tensor"),
        ),
        out_specs=(
            P("replica", "tensor", None),
            P("replica", "tensor", None),
            P("replica", "tensor", None),
            P("tensor", "replica"),
            P("tensor", "replica"),
            P("replica", "tensor", None),
        ),
        check_vma=False,
    )
```

profile of v0, /device:TPU:2, one launch (start us, length us, event | category | flops | bytes accessed | tf_op | source)
XLA Modules:
  0.0 434.6 jit_solution(7835340939217685011)
XLA Ops:
  8.0 0.0 copy-start
  8.0 0.0 all-reduce.2.cloned.1.call-start
  8.1 91.1 %all_gather.10 = f32[256,512]{0,1:T(8,128)S(1)} all-gather(f32[256,16]{0,1:T(8,128)} %param.13), channel_id=1, replica_groups=mesh['replica'=32,'tensor'=16] {'replica'}, dimensions={1}, use_global_device_ids=true | all-gather | bytes 540672 | tf_op jit(solution)/shard_map/all_gather | solution.py:63
  99.1 0.2 copy.30
  99.3 0.0 copy-done
  99.3 0.0 copy-start.1
  99.4 0.9 bitcast_subtract_fusion
  100.2 0.0 all-reduce.2.cloned.1.call-update
  100.2 0.0 all-gather.3.cloned.1.call-start
  100.3 0.5 all-gather.3.cloned.1.call-update
  100.8 0.0 reduce-scatter.2.cloned.1.call-start
  100.9 0.1 copy-done.1
  100.9 0.4 copy.35
  101.4 0.6 copy.27
  101.9 36.3 %all_to_all.19 = bf16[192,16,256]{2,0,1:T(8,128)(2,1)S(1)} all-to-all(bf16[192,16,256]{2,0,1:T(8,128)(2,1)S(1)} %copy.27), channel_id=1, replica_groups=mesh['replica'=32,'tensor'=16] {'tensor'}, dimensions={1} | all-to-all | bytes 3145728 | tf_op jit(solution)/shard_map/all_to_all | solution.py:35
  138.2 3.6 convolution_multiply_fusion
  141.9 0.0 copy-start.2
  141.9 0.0 reduce-scatter.2.cloned.1.call-update
  141.9 0.0 copy-start.3
  141.9 0.7 copy-done.2
  142.6 79.2 %all_gather.11 = f32[256,512]{0,1:T(8,128)S(1)} all-gather(f32[256,16]{0,1:T(8,128)S(1)} %copy-done.2), channel_id=1, replica_groups=mesh['replica'=32,'tensor'=16] {'replica'}, dimensions={1}, use_global_device_ids=true | all-gather | bytes 540672 | tf_op jit(solution)/shard_map/all_gather | solution.py:64
  221.8 1.0 copy.29
  222.8 0.0 copy-done.3
  222.8 195.2 %all-reduce.2.cloned.1.call-done = f32[256,512]{1,0:T(8,128)} async-done(((f32[256,512]{1,0:T(8,128)}), f32[256,512]{1,0:T(8,128)}) %all-reduce.2.cloned.1.call-update) | async-done | bytes 524304 | tf_op jit(solution)/shard_map/psum | solution.py:66
  417.9 0.0 all-gather.3.cloned.1.call-done
  417.9 5.1 %select_bitcast_fusion = (f32[1,256,512]{2,1,0:T(8,128)}, f32[256,512]{1,0:T(8,128)S(1)}, f32[256,512]{1,0:T(8,128)S(1)}, f32[1,256,512]{2,1,0:T(8,128)}, f32[1,256,512]{2,1,0:T(8,128)}) fusion(f32[1,256,512]{2,1,0:T(8,128)S(1)} %copy-done, pred[256]{0:T(512)(128)(4,1)S(1)} %broadcast_compare_fusion, f32[1,256,512]{2,1,0:T(8,128)} %param.11, ...), kind=kOutput, calls=%fused_computation.11 | convolution fusion | flops 808845312 | bytes 10486016 | tf_op jit(solution)/shard_map/dot_general | solution.py:45
  423.0 1.1 dynamic-slice_select_fusion
  424.2 0.7 copy.34
  424.8 0.7 copy.33
  425.5 0.0 reduce-scatter.2.cloned.1.call-done
  425.5 1.7 convert_bitcast_fusion
  (1 shorter events, 0.0 us)
Async XLA Ops:
  8.0 91.3 %copy-start = (f32[1,256,512]{2,1,0:T(8,128)S(1)}, f32[1,256,512]{2,1,0:T(8,128)}, u32[]{:S(2)}) copy-start(f32[1,256,512]{2,1,0:T(8,128)} %param.10) | copy-start | bytes 1572868
  8.0 409.9 %all-reduce.2.cloned.1.call-start = ((), (), s32[]{:S(2)}) async-start(), calls=%async_computation.2 | async-start | bytes 1048576 | tf_op jit(solution)/shard_map/psum | solution.py:66
  99.3 1.6 copy-start.1
  100.2 317.7 %all-gather.3.cloned.1.call-start = ((), (), s32[]{:S(2)}) async-start(), calls=%async_computation.4 | async-start | bytes 3342336 | tf_op jit(solution)/shard_map/all_gather | solution.py:47
  100.8 324.7 %reduce-scatter.2.cloned.1.call-start = ((), (), s32[]{:S(2)}) async-start(), calls=%async_computation.3 | async-start | bytes 6684672 | tf_op jit(solution)/shard_map/reduce_scatter | solution.py:37
  141.9 0.7 copy-start.2
  141.9 80.9 %copy-start.3 = (s32[256]{0:T(256)S(1)}, s32[256]{0:T(256)}, u32[]{:S(2)}) copy-start(s32[256]{0:T(256)} %param.15) | copy-start | bytes 3076
Sparse Core Ops, SparseCore 0:
  100.4 317.5 all-reduce.1
Sparse Core Ops, SparseCore 1:
  103.1 46.5 all-gather.2
  152.6 87.0 reduce-scatter.1
where the time goes:
time: 435 us
  blocking collectives  207 us (48%)
  waiting for transfers between devices  196 us (45%)
  between operations  15.6 us (4%)
  matrix products  8.75 us (2%)
    psum x1, waiting for transfers between devices, body(): summed_drift = lax.psum(full_anchor - weight_here, 'replica')  195 us
    all_gather x1, blocking collectives, body(): lax.all_gather(anchor, 'replica', axis=1, tiled=True)  91.1 us
    all_gather x1, blocking collectives, body(): lax.all_gather(outer_momentum, 'replica', axis=1, tiled=True)  79.2 us
    all_to_all x1, blocking collectives, body(): lax.all_to_all(inputs_here, 'tensor', split_axis=1, concat_axis=0, tiled=...  36.3 us
  transfers between devices with their start and end apart: 3, of which 1 were waited for; matrix products, arithmetic and copies ran while one was open for 3% of the time, Pallas kernels for 0%

commit v1 on v0

v1 whole, which is shorter than its diff:
```python
import jax
import jax.numpy as jnp
from jax import lax
from jax.experimental import pallas as pl
from jax.experimental.pallas import tpu as pltpu
from jax.sharding import PartitionSpec as P

D = 4096
C = 512
STEP = 20
NX = 4
NY = 8
NH = 4
ROWS = 256
TOK = 192
COLS = 16

FIRST_DECAY = 0.9
SECOND_DECAY = 0.95
ADAM_EPS = 1e-08
INNER_RATE = 0.02
WEIGHT_DECAY = 0.1
OUTER_RATE = 0.7
OUTER_MU = 0.9
MIX_SHARE = 0.5

BF = jnp.bfloat16
F32 = jnp.float32
MESH = pl.DeviceIdType.MESH


def kernel(
    act,
    cot,
    w_hbm,
    anchor,
    mom,
    frag,
    g_out,
    y_out,
    a_out,
    anchor_out,
    mom_out,
    w32,
    xq,
    cq,
    wq,
    acc,
    g_send,
    g_opp,
    g_sum,
    g_dir,
    y_send,
    y_sib,
    y_mid,
    y_far,
    wt,
    ybuf,
    s32,
    s16,
    zbuf,
    at,
    local_sem,
    x_send,
    x_recv,
    c_send,
    c_recv,
    w_send,
    w_recv,
    gs_send,
    gs_recv,
    ys_send,
    ys_recv,
    r_send,
    r_recv,
    h_send,
    h_recv,
    b_send,
    b_recv,
    a_send,
    a_recv,
):
    rep = lax.axis_index("replica")
    ten = lax.axis_index("tensor")
    y, h = rep // NH, rep % NH
    x, q = ten // 4, ten % 4
    z, c = q // 2, q % 2
    s = 1 - 2 * c

    def quad(zz, cc):
        return zz * 2 + cc

    others = ((z, 1 - c), (1 - z, c), (1 - z, 1 - c))
    q_sib, q_far, q_diag = (quad(*o) for o in others)
    ahead = (x + s + NX) % NX
    behind = (x - s + NX) % NX
    sib = (rep, x * 4 + q_sib)
    far = (rep, x * 4 + q_far)
    diag = (rep, x * 4 + q_diag)
    dev_ahead = (rep, ahead * 4 + q)
    dev_behind = (rep, behind * 4 + q)

    def y_dev(d):
        return (((y + d) % NY) * NH + h, ten)

    def h_dev(d):
        return (y * NH + (h + d) % NH, ten)

    peers = [sib, far, diag, dev_ahead, dev_behind]
    peers += [y_dev(d) for d in range(1, NY)] + [h_dev(d) for d in range(1, NH)]

    def remote(src, dst, send, recv, dev):
        return pltpu.make_async_remote_copy(
            src_ref=src, dst_ref=dst, send_sem=send, recv_sem=recv, device_id=dev, device_id_type=MESH
        )

    def rows(i, n=TOK):
        return pl.ds(pl.multiple_of(i * n, n if n % 16 else 16), n)

    def rows_tok(i):
        return pl.ds(pl.multiple_of(i * TOK, TOK), TOK)

    def x_block(cc, qq, j):
        ss = 1 - 2 * cc
        shift = (2, ss + NX, NX - ss, 0)[j]
        k = ((x + shift) % NX) * 4 + qq
        return act.at[:, pl.ds(pl.multiple_of(k * ROWS, ROWS), ROWS)]

    w_copy = pltpu.make_async_copy(w_hbm, w32, local_sem.at[0])
    w_copy.start()
    c_copy = pltpu.make_async_copy(cot, cq.at[rows_tok(q)], local_sem.at[1])
    c_copy.start()
    x_copies = [
        pltpu.make_async_copy(x_block(c, q, j), xq.at[j, rows_tok(q)], local_sem.at[2 + j]) for j in range(4)
    ]
    for copy in x_copies:
        copy.start()

    barrier = pltpu.get_barrier_semaphore()
    for dev in peers:
        pl.semaphore_signal(barrier, inc=1, device_id=dev, device_id_type=MESH)
    pl.semaphore_wait(barrier, len(peers))

    sends = []

    def start(copy):
        copy.start()
        sends.append(copy)
        return copy

    start(remote(cot, cq.at[rows_tok(q)], c_send.at[1], c_recv.at[1], far))
    start(remote(cot, cq.at[rows_tok(q)], c_send.at[0], c_recv.at[0], sib))
    for j in range(4):
        for e, (dev, (zz, cc)) in ((1, (far, others[1])), (2, (diag, others[2])), (0, (sib, others[0]))):
            start(
                remote(
                    x_block(cc, quad(zz, cc), j), xq.at[j, rows_tok(q)], x_send.at[j, e], x_recv.at[j, e], dev
                )
            )

    def x_wait(j):
        x_copies[j].wait()
        for e, qq in enumerate((q_sib, q_far, q_diag)):
            remote(act.at[:, pl.ds(0, ROWS)], xq.at[j, rows_tok(qq)], x_send.at[j, e], x_recv.at[j, e], sib).wait_recv()

    w_copy.wait()
    wq[3] = w32[...].astype(BF)
    start(remote(wq.at[3], wq.at[2], w_send.at[0], w_recv.at[2], dev_ahead))
    start(remote(wq.at[3], wq.at[1], w_send.at[1], w_recv.at[1], dev_behind))

    wt[...] = w32[...].T.astype(BF)
    for d in range(1, NY):
        to = (y + d) % NY
        start(remote(wt.at[pl.ds(pl.multiple_of(to * 64, 64), 64)], ybuf.at[d], r_send.at[d], r_recv.at[d], y_dev(d)))

    remote(cot, cq.at[rows_tok(q_far)], c_send.at[1], c_recv.at[1], far).wait_recv()
    start(remote(cq.at[rows_tok(q_far)], cq.at[rows_tok(q_far)], c_send.at[2], c_recv.at[2], sib))
    remote(wq.at[3], wq.at[2], w_send.at[0], w_recv.at[2], dev_ahead).wait_recv()
    start(remote(wq.at[2], wq.at[0], w_send.at[2], w_recv.at[0], dev_ahead))

    total = wt[pl.ds(pl.multiple_of(y * 64, 64), 64), :].astype(F32)
    for d in range(1, NY):
        remote(wt.at[pl.ds(0, 64)], ybuf.at[d], r_send.at[d], r_recv.at[d], y_dev(d)).wait_recv()
        total = total + ybuf[d].astype(F32)
    s32[...] = total
    s16[...] = total.astype(BF)
    for d in range(1, NH):
        to = (h + d) % NH
        start(remote(s16.at[pl.ds(pl.multiple_of(to * COLS, COLS), COLS)], zbuf.at[d], h_send.at[d], h_recv.at[d], h_dev(d)))

    remote(cot, cq.at[rows_tok(q_sib)], c_send.at[0], c_recv.at[0], sib).wait_recv()
    remote(cot, cq.at[rows_tok(q_diag)], c_send.at[2], c_recv.at[2], sib).wait_recv()
    c_copy.wait()

    def grad(j):
        return lax.dot_general(xq[j], cq[...], (((0,), (0,)), ((), ())), preferred_element_type=F32)

    def project(j):
        return jnp.dot(xq[j], wq[j], preferred_element_type=F32)

    x_wait(0)
    g_send[0] = grad(0).astype(BF)
    start(remote(g_send.at[0], g_opp, gs_send.at[0], gs_recv.at[0], dev_ahead))

    mine = pl.ds(pl.multiple_of(h * COLS, COLS), COLS)
    total = s32[mine, :]
    for d in range(1, NH):
        remote(s16.at[pl.ds(0, COLS)], zbuf.at[d], h_send.at[d], h_recv.at[d], h_dev(d)).wait_recv()
        total = total + zbuf[d].astype(F32)
    old = anchor[...]
    old_mom = mom[...]
    inside = frag[...] == 1
    pseudo = old - total * (1.0 / (NY * NH))
    new_mom = OUTER_MU * old_mom + pseudo
    new_anchor = jnp.where(inside, old - OUTER_RATE * (pseudo + OUTER_MU * new_mom), old)
    anchor_out[...] = new_anchor
    mom_out[...] = jnp.where(inside, new_mom, old_mom)
    my_rows = pl.ds(pl.multiple_of(rep * COLS, COLS), COLS)
    at[my_rows, :] = new_anchor.astype(BF)
    for d in range(1, NH):
        start(remote(at.at[my_rows], at.at[my_rows], b_send.at[d], b_recv.at[d], h_dev(d)))

    remote(wq.at[2], wq.at[0], w_send.at[2], w_recv.at[0], dev_ahead).wait_recv()
    acc[...] = project(0)

    x_wait(1)
    g = grad(1)
    remote(g_send.at[0], g_opp, gs_send.at[0], gs_recv.at[0], dev_ahead).wait_recv()
    g_send[1] = (g + g_opp[...].astype(F32)).astype(BF)
    start(remote(g_send.at[1], g_sum, gs_send.at[1], gs_recv.at[1], dev_ahead))

    for d in range(1, NH):
        src = pl.ds(pl.multiple_of((y * NH + (h - d + NH) % NH) * COLS, COLS), COLS)
        remote(at.at[src], at.at[src], b_send.at[d], b_recv.at[d], h_dev(d)).wait_recv()
    y_rows = pl.ds(pl.multiple_of(y * 64, 64), 64)
    for d in range(1, NY):
        start(remote(at.at[y_rows], at.at[y_rows], a_send.at[d], a_recv.at[d], y_dev(d)))

    remote(wq.at[3], wq.at[1], w_send.at[1], w_recv.at[1], dev_behind).wait_recv()
    acc[...] += project(1)

    x_wait(2)
    g_send[2] = grad(2).astype(BF)
    start(remote(g_send.at[2], g_dir, gs_send.at[2], gs_recv.at[2], dev_behind))
    acc[...] += project(2)

    for d in range(1, NY):
        src = pl.ds(pl.multiple_of(((y - d + NY) % NY) * 64, 64), 64)
        remote(at.at[src], at.at[src], a_send.at[d], a_recv.at[d], y_dev(d)).wait_recv()
    a_out[...] = at[...].astype(F32).T.astype(BF)

    x_wait(3)
    acc[...] += project(3)
    y_send[0] = acc[rows_tok(q_diag), :].astype(BF)
    start(remote(y_send.at[0], y_mid, ys_send.at[0], ys_recv.at[0], sib))
    y_send[1] = acc[rows_tok(q_sib), :].astype(BF)
    start(remote(y_send.at[1], y_sib, ys_send.at[1], ys_recv.at[1], sib))
    g = grad(3)
    remote(y_send.at[0], y_mid, ys_send.at[0], ys_recv.at[0], sib).wait_recv()
    y_send[2] = (acc[rows_tok(q_far), :] + y_mid[...].astype(F32)).astype(BF)
    start(remote(y_send.at[2], y_far, ys_send.at[2], ys_recv.at[2], far))
    remote(g_send.at[1], g_sum, gs_send.at[1], gs_recv.at[1], dev_ahead).wait_recv()
    g = g + g_sum[...].astype(F32)
    remote(g_send.at[2], g_dir, gs_send.at[2], gs_recv.at[2], dev_behind).wait_recv()
    g_out[...] = g + g_dir[...].astype(F32)

    remote(y_send.at[1], y_sib, ys_send.at[1], ys_recv.at[1], sib).wait_recv()
    total = acc[rows_tok(q), :] + y_sib[...].astype(F32)
    remote(y_send.at[2], y_far, ys_send.at[2], ys_recv.at[2], far).wait_recv()
    y_out[...] = ((total + y_far[...].astype(F32)) * D ** (-0.5)).astype(BF)

    for copy in sends:
        copy.wait_send()


def body(
    activations,
    cotangent,
    weight,
    first_moment,
    second_moment,
    anchor,
    outer_momentum,
    fragment_rows,
):
    weight_here = weight[0]
    vmem = pl.BlockSpec(memory_space=pltpu.VMEM)
    hbm = pl.BlockSpec(memory_space=pl.ANY)
    dma = pltpu.SemaphoreType.DMA
    gradient, projected, anchor_full, anchor_new, momentum_new = pl.pallas_call(
        kernel,
        out_shape=(
            jax.ShapeDtypeStruct((ROWS, C), F32),
            jax.ShapeDtypeStruct((TOK, C), BF),
            jax.ShapeDtypeStruct((ROWS, C), BF),
            jax.ShapeDtypeStruct((COLS, ROWS), F32),
            jax.ShapeDtypeStruct((COLS, ROWS), F32),
        ),
        in_specs=[hbm, hbm, hbm, vmem, vmem, vmem],
        out_specs=[vmem] * 5,
        scratch_shapes=[
            pltpu.VMEM((ROWS, C), F32),
            pltpu.VMEM((4, 4 * TOK, ROWS), BF),
            pltpu.VMEM((4 * TOK, C), BF),
            pltpu.VMEM((4, ROWS, C), BF),
            pltpu.VMEM((4 * TOK, C), F32),
            pltpu.VMEM((3, ROWS, C), BF),
            pltpu.VMEM((ROWS, C), BF),
            pltpu.VMEM((ROWS, C), BF),
            pltpu.VMEM((ROWS, C), BF),
            pltpu.VMEM((3, TOK, C), BF),
            pltpu.VMEM((TOK, C), BF),
            pltpu.VMEM((TOK, C), BF),
            pltpu.VMEM((TOK, C), BF),
            pltpu.VMEM((C, ROWS), BF),
            pltpu.VMEM((NY, 64, ROWS), BF),
            pltpu.VMEM((64, ROWS), F32),
            pltpu.VMEM((64, ROWS), BF),
            pltpu.VMEM((NH, COLS, ROWS), BF),
            pltpu.VMEM((C, ROWS), BF),
            dma((6,)),
            dma((4, 3)),
            dma((4, 3)),
            dma((3,)),
            dma((3,)),
            dma((3,)),
            dma((3,)),
            dma((3,)),
            dma((3,)),
            dma((3,)),
            dma((3,)),
            dma((NY,)),
            dma((NY,)),
            dma((NH,)),
            dma((NH,)),
            dma((NH,)),
            dma((NH,)),
            dma((NY,)),
            dma((NY,)),
        ],
        compiler_params=pltpu.CompilerParams(
            collective_id=0, has_side_effects=True, vmem_limit_bytes=32 * 1024 * 1024
        ),
        name="exchange",
    )(
        activations[0],
        cotangent[0],
        weight_here,
        anchor.T,
        outer_momentum.T,
        fragment_rows[None, :],
    )
    gradient = gradient * D ** (-0.5)
    first_new = FIRST_DECAY * first_moment[0] + (1.0 - FIRST_DECAY) * gradient
    second_new = SECOND_DECAY * second_moment[0] + (1.0 - SECOND_DECAY) * gradient * gradient
    first_hat = first_new / (1.0 - FIRST_DECAY**STEP)
    second_hat = second_new / (1.0 - SECOND_DECAY**STEP)
    update = first_hat / (jnp.sqrt(second_hat) + ADAM_EPS) + WEIGHT_DECAY * weight_here
    inner = weight_here - INNER_RATE * update
    in_fragment = (fragment_rows == 1)[:, None]
    merged = (1.0 - MIX_SHARE) * inner + MIX_SHARE * anchor_full.astype(F32)
    weight_out = jnp.where(in_fragment, merged, inner)
    return (
        weight_out[None],
        first_new[None],
        second_new[None],
        anchor_new.T,
        momentum_new.T,
        projected[None],
    )


def solution(mesh):
    return jax.shard_map(
        body,
        mesh=mesh,
        in_specs=(
            P("replica", "tensor", None),
            P("replica", "tensor", None),
            P("replica", "tensor", None),
            P("replica", "tensor", None),
            P("replica", "tensor", None),
            P("tensor", "replica"),
            P("tensor", "replica"),
            P("tensor"),
        ),
        out_specs=(
            P("replica", "tensor", None),
            P("replica", "tensor", None),
            P("replica", "tensor", None),
            P("tensor", "replica"),
            P("tensor", "replica"),
            P("replica", "tensor", None),
        ),
        check_vma=False,
    )
```

time: 435 us -> 70.3 us (0.16)
  the two profiles are of different devices: /device:TPU:2 before, /device:TPU:1 now
where the time goes in v1:
time: 70.3 us; the launch traced here: 70 us
  Pallas kernels  59.6 us (85%)
  local copies, waits for them, and re-layouts  7.38 us (10%)
  other arithmetic  2.31 us (3%)
    pallas_call x1, Pallas kernels, body(): pl.pallas_call(kernel, out_shape=(jax.ShapeDtypeStruct((ROWS, C), F32), j...  59.6 us
    unnamed x19, local copies, waits for them, and re-layouts  7.38 us
    broadcast_in_dim x1, other arithmetic, body(): second_new[None]  1.62 us

profile of v1, /device:TPU:1, one launch (start us, length us, event | category | flops | bytes accessed | tf_op | source)
XLA Modules:
  0.0 70.0 jit_solution(1891801914023558544)
XLA Ops:
  0.6 0.7 broadcast_compare_fusion
  1.3 0.0 copy-start
  1.3 1.0 %copy-done = f32[1,256,512]{2,1,0:T(8,128)S(1)} copy-done((f32[1,256,512]{2,1,0:T(8,128)S(1)}, f32[1,256,512]{2,1,0:T(8,128)}, u32[]{:S(2)}) %copy-start) | copy-done | bytes 524312
  2.4 0.0 copy-start.1
  2.4 1.4 %copy-done.1 = bf16[1,192,4096]{2,1,0:T(8,128)(2,1)S(1)} copy-done((bf16[1,192,4096]{2,1,0:T(8,128)(2,1)S(1)}, bf16[1,192,4096]{2,1,0:T(8,128)(2,1)}, u32[]{:S(2)}) %copy-start.1) | copy-done | bytes 1572888
  3.8 0.0 copy-start.2
  3.8 0.9 %copy-done.2 = bf16[1,192,512]{2,1,0:T(8,128)(2,1)S(1)} copy-done((bf16[1,192,512]{2,1,0:T(8,128)(2,1)S(1)}, bf16[1,192,512]{2,1,0:T(8,128)(2,1)}, u32[]{:S(2)}) %copy-start.2) | copy-done | bytes 196632
  4.7 0.0 copy-start.3
  4.7 0.7 %copy-done.3 = f32[256,16]{0,1:T(8,128)S(1)} copy-done((f32[256,16]{0,1:T(8,128)S(1)}, f32[256,16]{0,1:T(8,128)}, u32[]{:S(2)}) %copy-start.3) | copy-done | bytes 16408
  5.4 0.0 copy-start.4
  5.4 0.7 %copy-done.4 = f32[256,16]{0,1:T(8,128)S(1)} copy-done((f32[256,16]{0,1:T(8,128)S(1)}, f32[256,16]{0,1:T(8,128)}, u32[]{:S(2)}) %copy-start.4) | copy-done | bytes 16408
  6.1 0.0 copy-start.5
  6.1 0.7 copy-done.5
  6.8 0.0 copy-start.6
  6.8 0.0 copy-start.7
  6.8 59.6 %exchange.1 = (f32[256,512]{1,0:T(8,128)S(1)}, bf16[192,512]{1,0:T(8,128)(2,1)S(1)}, bf16[256,512]{1,0:T(8,128)(2,1)S(1)}, f32[16,256]{1,0:T(8,128)S(1)}, f32[16,256]{1,0:T(8,128)S(1)}) custom-call(bf16[192,4096]{1,0:T(8,128)(2,1)S(1)} %bitcast.29, bf16[192,512]{1,0:T(8,128)(2,1)S(1)} %bitcast.30, f32[256,512]{1,0:T(8,128)S(1)} %bitcast.28, ...), custom_call_target="tpu_custom_call" | custom-call | tf_op jit(solution)/shard_map/exchange/pallas_call | solution.py:290
  66.5 0.0 copy-done.6
  66.5 0.0 copy-done.7
  66.5 1.6 %fusion.1 = (f32[1,256,512]{2,1,0:T(8,128)}, f32[1,256,512]{2,1,0:T(8,128)}, f32[1,256,512]{2,1,0:T(8,128)}) fusion(f32[256,512]{1,0:T(8,128)S(1)} %get-tuple-element.11, f32[1,256,512]{2,1,0:T(8,128)S(1)} %copy-done.6, bf16[256,512]{1,0:T(8,128)(2,1)S(1)} %get-tuple-element.12, f32[1,256,512]{2,1,0:T(8,128)S(1)} %copy-done.7, f32[1,256,512]{2,1,0:T(8,128)S(1)} %copy-done, ...), kind=kLoop, calls=%fused_computation.4 | loop fusion | flops 2621440 | bytes 3932416 | tf_op jit(solution)/shard_map/broadcast_in_dim | solution.py:366
  68.1 0.6 copy.17
  68.7 0.6 copy.18
  69.3 0.7 copy.19
Async XLA Ops:
  1.3 1.0 %copy-start = (f32[1,256,512]{2,1,0:T(8,128)S(1)}, f32[1,256,512]{2,1,0:T(8,128)}, u32[]{:S(2)}) copy-start(f32[1,256,512]{2,1,0:T(8,128)} %param.10) | copy-start | bytes 1572868
  2.4 1.4 %copy-start.1 = (bf16[1,192,4096]{2,1,0:T(8,128)(2,1)S(1)}, bf16[1,192,4096]{2,1,0:T(8,128)(2,1)}, u32[]{:S(2)}) copy-start(bf16[1,192,4096]{2,1,0:T(8,128)(2,1)} %param.8) | copy-start | bytes 4718596
  3.8 0.9 %copy-start.2 = (bf16[1,192,512]{2,1,0:T(8,128)(2,1)S(1)}, bf16[1,192,512]{2,1,0:T(8,128)(2,1)}, u32[]{:S(2)}) copy-start(bf16[1,192,512]{2,1,0:T(8,128)(2,1)} %param.9) | copy-start | bytes 589828
  4.7 0.7 %copy-start.3 = (f32[256,16]{0,1:T(8,128)S(1)}, f32[256,16]{0,1:T(8,128)}, u32[]{:S(2)}) copy-start(f32[256,16]{0,1:T(8,128)} %param.13) | copy-start | bytes 49156
  5.4 0.7 %copy-start.4 = (f32[256,16]{0,1:T(8,128)S(1)}, f32[256,16]{0,1:T(8,128)}, u32[]{:S(2)}) copy-start(f32[256,16]{0,1:T(8,128)} %param.14) | copy-start | bytes 49156
  6.1 0.7 copy-start.5
  6.8 59.7 %copy-start.6 = (f32[1,256,512]{2,1,0:T(8,128)S(1)}, f32[1,256,512]{2,1,0:T(8,128)}, u32[]{:S(2)}) copy-start(f32[1,256,512]{2,1,0:T(8,128)} %param.12) | copy-start | bytes 1572868
  6.8 59.7 %copy-start.7 = (f32[1,256,512]{2,1,0:T(8,128)S(1)}, f32[1,256,512]{2,1,0:T(8,128)}, u32[]{:S(2)}) copy-start(f32[1,256,512]{2,1,0:T(8,128)} %param.11) | copy-start | bytes 1572868

commit v2 on v1

v2 whole, which is shorter than its diff:
```python
import jax
import jax.numpy as jnp
from jax import lax
from jax.experimental import pallas as pl
from jax.experimental.pallas import tpu as pltpu
from jax.sharding import PartitionSpec as P

D = 4096
C = 512
STEP = 20
NX = 4
NY = 8
NH = 4
ROWS = 256
TOK = 192
HALF = TOK // 2
COLS = 16
BAND = NH * COLS
SCALE = D ** (-0.5)

FIRST_DECAY = 0.9
SECOND_DECAY = 0.95
ADAM_EPS = 1e-08
INNER_RATE = 0.02
WEIGHT_DECAY = 0.1
OUTER_RATE = 0.7
OUTER_MU = 0.9
MIX_SHARE = 0.5

BF = jnp.bfloat16
F32 = jnp.float32
MESH = pl.DeviceIdType.MESH
AHEAD = 3


def exchange(
    act,
    cot,
    weight,
    anchor,
    mom,
    frag,
    first,
    second,
    w_out,
    first_out,
    second_out,
    anchor_out,
    mom_out,
    y_out,
    w32,
    f32,
    v32,
    old_anchor,
    old_mom,
    frag_v,
    xq,
    cq,
    wq,
    acc,
    g_send,
    g_opp,
    g_sum,
    g_dir,
    g_res,
    ym_out,
    ym_in,
    ys_out,
    ys_in,
    yf_out,
    yf_in,
    y_res,
    wt,
    ybuf,
    s32,
    s16,
    zbuf,
    at,
    a_res,
    m_res,
    new_anchor,
    new_mom,
    local_sem,
    out_sem,
    x_send,
    x_recv,
    c_send,
    c_recv,
    w_send,
    w_recv,
    gs_send,
    gs_recv,
    ym_send,
    ym_recv,
    ys_send,
    ys_recv,
    yf_send,
    yf_recv,
    r_send,
    r_recv,
    h_send,
    h_recv,
    b_send,
    b_recv,
    a_send,
    a_recv,
):
    rep = lax.axis_index("replica")
    ten = lax.axis_index("tensor")
    y, h = rep // NH, rep % NH
    x, q = ten // 4, ten % 4
    z, c = q // 2, q % 2
    s = 1 - 2 * c

    others = ((z, 1 - c), (1 - z, c), (1 - z, 1 - c))
    q_sib, q_far, q_diag = (zz * 2 + cc for zz, cc in others)
    ahead = (x + s + NX) % NX
    behind = (x - s + NX) % NX
    sib = (rep, x * 4 + q_sib)
    far = (rep, x * 4 + q_far)
    diag = (rep, x * 4 + q_diag)
    dev_ahead = (rep, ahead * 4 + q)
    dev_behind = (rep, behind * 4 + q)

    def y_dev(d):
        return (((y + d) % NY) * NH + h, ten)

    def h_dev(d):
        return (y * NH + (h + d) % NH, ten)

    peers = [sib, far, diag, dev_ahead, dev_behind]
    peers += [y_dev(d) for d in range(1, NY)] + [h_dev(d) for d in range(1, NH)]
    barrier = pltpu.get_barrier_semaphore()
    for dev in peers:
        pl.semaphore_signal(barrier, inc=1, device_id=dev, device_id_type=MESH)

    def remote(src, dst, send, recv, dev):
        return pltpu.make_async_remote_copy(
            src_ref=src, dst_ref=dst, send_sem=send, recv_sem=recv, device_id=dev, device_id_type=MESH
        )

    def part(i, n):
        return pl.ds(pl.multiple_of(i * n, n), n)

    def halves(qq, k):
        return pl.ds(pl.multiple_of(qq * TOK + k * HALF, HALF), HALF)

    def x_cols(cc, qq, j):
        ss = 1 - 2 * cc
        shift = (2, ss + NX, NX - ss, 0)[j]
        return part(((x + shift) % NX) * 4 + qq, ROWS)

    def local(src, dst, sem):
        copy = pltpu.make_async_copy(src, dst, sem)
        copy.start()
        return copy

    w_copy = local(weight, w32, local_sem.at[0])
    c_copy = local(cot, cq.at[part(q, TOK)], local_sem.at[1])
    x_copies = [local(act.at[:, x_cols(c, q, j)], xq.at[j, part(q, TOK)], local_sem.at[2 + j]) for j in range(4)]
    small_copies = [
        local(anchor, old_anchor, local_sem.at[6]),
        local(mom, old_mom, local_sem.at[7]),
        local(frag, frag_v, local_sem.at[8]),
    ]
    moment_copies = [local(first, f32, local_sem.at[9]), local(second, v32, local_sem.at[10])]

    w_copy.wait()
    wt[...] = w32[...].T.astype(BF)
    wq[3] = w32[...].astype(BF)
    for copy in small_copies:
        copy.wait()
    m_res[...] = jnp.broadcast_to((frag_v[...] == 1).astype(F32), (128, ROWS)).T

    pl.semaphore_wait(barrier, len(peers))

    sends = []

    def start(copy):
        copy.start()
        sends.append(copy)
        return copy

    stage_r = {}
    for d in range(1, NY):
        stage_r[d] = start(
            remote(wt.at[part((y + d) % NY, BAND)], ybuf.at[d], r_send.at[d], r_recv.at[d], y_dev(d))
        )

    w_ahead = start(remote(wq.at[3], wq.at[2], w_send.at[0], w_recv.at[0], dev_ahead))
    w_behind = start(remote(wq.at[3], wq.at[1], w_send.at[1], w_recv.at[1], dev_behind))
    start(remote(cot, cq.at[part(q, TOK)], c_send.at[1], c_recv.at[1], far))
    start(remote(cot, cq.at[part(q, TOK)], c_send.at[0], c_recv.at[0], sib))
    targets = ((1, far, others[1]), (2, diag, others[2]), (0, sib, others[0]))

    def x_issue(u):
        j, k = u // 2, u % 2
        for e, dev, (zz, cc) in targets:
            src = act.at[pl.ds(k * HALF, HALF), x_cols(cc, zz * 2 + cc, j)]
            start(remote(src, xq.at[j, halves(q, k)], x_send.at[u, e], x_recv.at[u, e], dev))

    def x_wait(u):
        j, k = u // 2, u % 2
        if k == 0:
            x_copies[j].wait()
        for e, qq in enumerate((q_sib, q_far, q_diag)):
            src = act.at[pl.ds(0, HALF), pl.ds(0, ROWS)]
            remote(src, xq.at[j, halves(qq, k)], x_send.at[u, e], x_recv.at[u, e], sib).wait_recv()
        if u + AHEAD < 8:
            x_issue(u + AHEAD)

    for u in range(AHEAD):
        x_issue(u)

    w_ahead.wait_recv()
    w_pass = start(remote(wq.at[2], wq.at[0], w_send.at[2], w_recv.at[2], dev_ahead))
    remote(cot, cq.at[part(q_far, TOK)], c_send.at[1], c_recv.at[1], far).wait_recv()
    start(remote(cq.at[part(q_far, TOK)], cq.at[part(q_far, TOK)], c_send.at[2], c_recv.at[2], sib))

    def grad(j):
        return lax.dot_general(xq[j], cq[...], (((0,), (0,)), ((), ())), preferred_element_type=F32)

    def project(j):
        return jnp.dot(xq[j], wq[j], preferred_element_type=F32)

    x_wait(0)

    total = wt[part(y, BAND), :].astype(F32)
    for d in range(1, NY):
        stage_r[d].wait_recv()
        total = total + ybuf[d].astype(F32)
    s32[...] = total
    s16[...] = total.astype(BF)
    stage_h = {}
    for d in range(1, NH):
        stage_h[d] = start(remote(s16.at[part((h + d) % NH, COLS)], zbuf.at[d], h_send.at[d], h_recv.at[d], h_dev(d)))

    x_wait(1)
    remote(cot, cq.at[part(q_sib, TOK)], c_send.at[0], c_recv.at[0], sib).wait_recv()
    remote(cot, cq.at[part(q_diag, TOK)], c_send.at[2], c_recv.at[2], sib).wait_recv()
    c_copy.wait()
    g_send[0] = grad(0).astype(BF)
    to_opp = start(remote(g_send.at[0], g_opp, gs_send.at[0], gs_recv.at[0], dev_ahead))

    mine = part(h, COLS)
    total = s32[mine, :]
    for d in range(1, NH):
        stage_h[d].wait_recv()
        total = total + zbuf[d].astype(F32)
    inside = frag_v[...] == 1
    pseudo = old_anchor[...] - total * (1.0 / (NY * NH))
    momentum = OUTER_MU * old_mom[...] + pseudo
    moved = old_anchor[...] - OUTER_RATE * (pseudo + OUTER_MU * momentum)
    at[part(rep, COLS), :] = jnp.where(inside, MIX_SHARE * moved, 0.0).astype(BF)
    for d in range(1, NH):
        start(remote(at.at[part(rep, COLS)], at.at[part(rep, COLS)], b_send.at[d], b_recv.at[d], h_dev(d)))
    new_anchor[...] = jnp.where(inside, moved, old_anchor[...])
    new_mom[...] = jnp.where(inside, momentum, old_mom[...])
    outs = [local(new_anchor, anchor_out, out_sem.at[0]), local(new_mom, mom_out, out_sem.at[1])]

    x_wait(2)
    w_pass.wait_recv()
    acc[...] = project(0)

    x_wait(3)
    g = grad(1)
    to_opp.wait_recv()
    g_send[1] = (g + g_opp[...].astype(F32)).astype(BF)
    to_ahead = start(remote(g_send.at[1], g_sum, gs_send.at[1], gs_recv.at[1], dev_ahead))

    for d in range(1, NH):
        theirs = part(y * NH + (h - d + NH) % NH, COLS)
        remote(at.at[theirs], at.at[theirs], b_send.at[d], b_recv.at[d], h_dev(d)).wait_recv()
    for d in range(1, NY):
        start(remote(at.at[part(y, BAND)], at.at[part(y, BAND)], a_send.at[d], a_recv.at[d], y_dev(d)))

    x_wait(4)
    w_behind.wait_recv()
    acc[...] += project(1)

    x_wait(5)
    g_send[2] = grad(2).astype(BF)
    to_behind = start(remote(g_send.at[2], g_dir, gs_send.at[2], gs_recv.at[2], dev_behind))
    acc[...] += project(2)

    def last(qq, k):
        return acc[halves(qq, k), :] + jnp.dot(xq[3, halves(qq, k), :], wq[3], preferred_element_type=F32)

    mids, sibs, fars = {}, {}, {}
    for k in range(2):
        x_wait(6 + k)
        ym_out[k] = last(q_diag, k).astype(BF)
        mids[k] = start(remote(ym_out.at[k], ym_in.at[k], ym_send.at[k], ym_recv.at[k], sib))
        ys_out[k] = last(q_sib, k).astype(BF)
        sibs[k] = start(remote(ys_out.at[k], ys_in.at[k], ys_send.at[k], ys_recv.at[k], sib))
        beyond = last(q_far, k)
        acc[halves(q, k), :] = last(q, k)
        mids[k].wait_recv()
        yf_out[k] = (beyond + ym_in[k].astype(F32)).astype(BF)
        fars[k] = start(remote(yf_out.at[k], yf_in.at[k], yf_send.at[k], yf_recv.at[k], far))

    g_res[...] = grad(3)
    for d in range(1, NY):
        theirs = part((y - d + NY) % NY, BAND)
        remote(at.at[theirs], at.at[theirs], a_send.at[d], a_recv.at[d], y_dev(d)).wait_recv()
    a_res[...] = at[...].astype(F32).T
    to_ahead.wait_recv()
    to_behind.wait_recv()
    for copy in moment_copies:
        copy.wait()

    def inner_step(i, carry):
        r = part(i, 32)
        gradient = (g_res[r, :] + g_sum[r, :].astype(F32) + g_dir[r, :].astype(F32)) * SCALE
        moment = FIRST_DECAY * f32[r, :] + (1.0 - FIRST_DECAY) * gradient
        square = SECOND_DECAY * v32[r, :] + (1.0 - SECOND_DECAY) * gradient * gradient
        f32[r, :] = moment
        v32[r, :] = square
        first_hat = moment / (1.0 - FIRST_DECAY**STEP)
        second_hat = square / (1.0 - SECOND_DECAY**STEP)
        update = first_hat / (jnp.sqrt(second_hat) + ADAM_EPS) + WEIGHT_DECAY * w32[r, :]
        inner = w32[r, :] - INNER_RATE * update
        share = 1.0 - MIX_SHARE * m_res[r, :][:, :1]
        w32[r, :] = inner * share + a_res[r, :]
        return carry

    lax.fori_loop(0, ROWS // 32, inner_step, 0)
    outs += [
        local(w32, w_out, out_sem.at[2]),
        local(f32, first_out, out_sem.at[3]),
        local(v32, second_out, out_sem.at[4]),
    ]

    for k in range(2):
        sibs[k].wait_recv()
        fars[k].wait_recv()
        total = acc[halves(q, k), :] + ys_in[k].astype(F32) + yf_in[k].astype(F32)
        y_res[pl.ds(k * HALF, HALF), :] = (total * SCALE).astype(BF)
    outs.append(local(y_res, y_out, out_sem.at[5]))

    for copy in sends:
        copy.wait_send()
    for copy in outs:
        copy.wait()


def finish(*refs):
    sources, results, held, in_sem, out_sem = refs[:6], refs[6:12], refs[12:18], refs[18], refs[19]
    comes = [pltpu.make_async_copy(a, b, in_sem.at[i]) for i, (a, b) in enumerate(zip(sources, held))]
    goes = [pltpu.make_async_copy(a, b, out_sem.at[i]) for i, (a, b) in enumerate(zip(held, results))]
    for copy in comes:
        copy.start()
    for before, after in zip(comes, goes):
        before.wait()
        after.start()
    for copy in goes:
        copy.wait()


def body(
    activations,
    cotangent,
    weight,
    first_moment,
    second_moment,
    anchor,
    outer_momentum,
    fragment_rows,
):
    hbm = pl.BlockSpec(memory_space=pltpu.HBM)
    free = pl.BlockSpec(memory_space=pl.ANY)
    dma = pltpu.SemaphoreType.DMA
    vm = pltpu.VMEM
    shape = jax.ShapeDtypeStruct
    out_shape = (
        shape((ROWS, C), F32),
        shape((ROWS, C), F32),
        shape((ROWS, C), F32),
        shape((COLS, ROWS), F32),
        shape((COLS, ROWS), F32),
        shape((TOK, C), BF),
    )
    results = pl.pallas_call(
        exchange,
        out_shape=out_shape,
        in_specs=[hbm] * 8,
        out_specs=[free] * 6,
        scratch_shapes=[
            vm((ROWS, C), F32),
            vm((ROWS, C), F32),
            vm((ROWS, C), F32),
            vm((COLS, ROWS), F32),
            vm((COLS, ROWS), F32),
            vm((1, ROWS), jnp.int32),
            vm((4, 4 * TOK, ROWS), BF),
            vm((4 * TOK, C), BF),
            vm((4, ROWS, C), BF),
            vm((4 * TOK, C), F32),
            vm((3, ROWS, C), BF),
            vm((ROWS, C), BF),
            vm((ROWS, C), BF),
            vm((ROWS, C), BF),
            vm((ROWS, C), F32),
            vm((2, HALF, C), BF),
            vm((2, HALF, C), BF),
            vm((2, HALF, C), BF),
            vm((2, HALF, C), BF),
            vm((2, HALF, C), BF),
            vm((2, HALF, C), BF),
            vm((TOK, C), BF),
            vm((C, ROWS), BF),
            vm((NY, BAND, ROWS), BF),
            vm((BAND, ROWS), F32),
            vm((BAND, ROWS), BF),
            vm((NH, COLS, ROWS), BF),
            vm((C, ROWS), BF),
            vm((ROWS, C), F32),
            vm((ROWS, 128), F32),
            vm((COLS, ROWS), F32),
            vm((COLS, ROWS), F32),
            dma((11,)),
            dma((6,)),
            dma((8, 3)),
            dma((8, 3)),
            dma((3,)),
            dma((3,)),
            dma((3,)),
            dma((3,)),
            dma((3,)),
            dma((3,)),
            dma((2,)),
            dma((2,)),
            dma((2,)),
            dma((2,)),
            dma((2,)),
            dma((2,)),
            dma((NY,)),
            dma((NY,)),
            dma((NH,)),
            dma((NH,)),
            dma((NH,)),
            dma((NH,)),
            dma((NY,)),
            dma((NY,)),
        ],
        compiler_params=pltpu.CompilerParams(
            collective_id=0, has_side_effects=True, vmem_limit_bytes=60 * 1024 * 1024
        ),
        name="exchange",
    )(
        activations[0],
        cotangent[0],
        weight[0],
        anchor.T,
        outer_momentum.T,
        fragment_rows[None, :],
        first_moment[0],
        second_moment[0],
    )

    weight_out, first_new, second_new, anchor_new, momentum_new, projected = pl.pallas_call(
        finish,
        out_shape=out_shape,
        in_specs=[hbm] * 6,
        out_specs=[hbm] * 6,
        scratch_shapes=[vm(a.shape, a.dtype) for a in out_shape] + [dma((6,))] * 2,
        compiler_params=pltpu.CompilerParams(vmem_limit_bytes=60 * 1024 * 1024),
        name="finish",
    )(*results)
    return (
        weight_out[None],
        first_new[None],
        second_new[None],
        anchor_new.T,
        momentum_new.T,
        projected[None],
    )


def solution(mesh):
    return jax.shard_map(
        body,
        mesh=mesh,
        in_specs=(
            P("replica", "tensor", None),
            P("replica", "tensor", None),
            P("replica", "tensor", None),
            P("replica", "tensor", None),
            P("replica", "tensor", None),
            P("tensor", "replica"),
            P("tensor", "replica"),
            P("tensor"),
        ),
        out_specs=(
            P("replica", "tensor", None),
            P("replica", "tensor", None),
            P("replica", "tensor", None),
            P("tensor", "replica"),
            P("tensor", "replica"),
            P("replica", "tensor", None),
        ),
        check_vma=False,
    )
```

time: 70.3 us -> 50.1 us (0.71)
  Pallas kernels: 59.6 us -> 49.3 us
  local copies, waits for them, and re-layouts: 7.38 us -> 0 us
  other arithmetic: 2.31 us -> 0 us
    pallas_call x1 -> x2, Pallas kernels: 59.6 us -> 49.3 us  [the longest x1 46.9 us: body(): pl.pallas_call(exchange, out_shape=out_shape, in_specs=[hbm] * 8, out_spe...]
    unnamed x19 -> x0, local copies, waits for them, and re-layouts: 7.38 us -> none
    broadcast_in_dim x1 -> x0, other arithmetic: 1.62 us -> none  [body(): second_new[None]]
where the time goes in v2:
time: 50.1 us; the launch traced here: 49.9 us
  Pallas kernels  49.3 us (98%)
  between operations  0.64 us (1%)
    pallas_call x1, Pallas kernels, body(): pl.pallas_call(exchange, out_shape=out_shape, in_specs=[hbm] * 8, out_spe...  46.9 us
    pallas_call x1, Pallas kernels, body(): pl.pallas_call(finish, out_shape=out_shape, in_specs=[hbm] * 6, out_specs...  2.35 us

profile of v2, /device:TPU:1, one launch (start us, length us, event | category | flops | bytes accessed | tf_op | source)
XLA Modules:
  0.0 49.9 jit_solution(2028648517113351285)
XLA Ops:
  0.6 46.9 %exchange.1 = (f32[256,512]{1,0:T(8,128)}, f32[256,512]{1,0:T(8,128)}, f32[256,512]{1,0:T(8,128)}, f32[16,256]{1,0:T(8,128)}, f32[16,256]{1,0:T(8,128)}, /*index=5*/bf16[192,512]{1,0:T(8,128)(2,1)}) custom-call(bf16[192,4096]{1,0:T(8,128)(2,1)} %bitcast.14, bf16[192,512]{1,0:T(8,128)(2,1)} %bitcast.18, f32[256,512]{1,0:T(8,128)} %bitcast.15, ...), custom_call_target="tpu_custom_call" | custom-call | tf_op jit(solution)/shard_map/exchange/pallas_call | solution.py:383
  47.5 2.4 %finish.1 = (f32[256,512]{1,0:T(8,128)}, f32[256,512]{1,0:T(8,128)}, f32[256,512]{1,0:T(8,128)}, f32[16,256]{1,0:T(8,128)}, f32[16,256]{1,0:T(8,128)}, /*index=5*/bf16[192,512]{1,0:T(8,128)(2,1)}) custom-call(f32[256,512]{1,0:T(8,128)} %get-tuple-element.18.refs_0_, f32[256,512]{1,0:T(8,128)} %get-tuple-element.19.refs_1_, ...), custom_call_target="tpu_custom_call" | custom-call | tf_op jit(solution)/shard_map/finish/pallas_call | solution.py:461

commit v3 on v2

v3 whole, which is shorter than its diff:
```python
import jax
import jax.numpy as jnp
from jax import lax
from jax.experimental import pallas as pl
from jax.experimental.pallas import tpu as pltpu
from jax.sharding import PartitionSpec as P

D = 4096
C = 512
STEP = 20
NX = 4
NY = 8
NH = 4
ROWS = 256
TOK = 192
CUT = 96
UNITS = TOK // CUT
COLS = 16
BAND = NH * COLS
SCALE = D ** (-0.5)

FIRST_DECAY = 0.9
SECOND_DECAY = 0.95
ADAM_EPS = 1e-08
INNER_RATE = 0.02
WEIGHT_DECAY = 0.1
OUTER_RATE = 0.7
OUTER_MU = 0.9
MIX_SHARE = 0.5

BF = jnp.bfloat16
F32 = jnp.float32
MESH = pl.DeviceIdType.MESH
AHEAD = 2
PLACES = (0, 2, 4)
PARTS = ((0, 96), (96, 96))


def exchange(
    act,
    cot,
    weight,
    anchor,
    mom,
    frag,
    first,
    second,
    w_out,
    first_out,
    second_out,
    anchor_out,
    mom_out,
    y_out,
    w32,
    f32,
    v32,
    old_anchor,
    old_mom,
    frag_v,
    xq,
    cq,
    wq,
    acc,
    g_send,
    g_opp,
    g_sum,
    g_dir,
    g_res,
    ym_out,
    ym_in,
    ys_out,
    ys_in,
    yf_out,
    yf_in,
    wt,
    ybuf,
    s32,
    s16,
    zbuf,
    at,
    m_res,
    local_sem,
    x_send,
    x_recv,
    c_send,
    c_recv,
    w_send,
    w_recv,
    gs_send,
    gs_recv,
    ym_send,
    ym_recv,
    ys_send,
    ys_recv,
    yf_send,
    yf_recv,
    r_send,
    r_recv,
    h_send,
    h_recv,
    b_send,
    b_recv,
    a_send,
    a_recv,
):
    rep = lax.axis_index("replica")
    ten = lax.axis_index("tensor")
    y, h = rep // NH, rep % NH
    x, z, c = ten // 4, (ten // 2) % 2, ten % 2
    pair = x // 2
    side = (x + pair) % 2
    place = pair + z * (3 - 2 * pair)
    q = side * 2 + c
    s = 1 - 2 * c

    def tensor_at(i, g, cc):
        zz = i // 2
        p = (i + zz) % 2
        return (g + p * (3 - 2 * g)) * 4 + zz * 2 + cc

    others = ((side, 1 - c), (1 - side, c), (1 - side, 1 - c))
    q_sib, q_far, q_diag = (g * 2 + cc for g, cc in others)
    sib, far, diag = ((rep, tensor_at(place, g, cc)) for g, cc in others)
    dev_ahead = (rep, tensor_at((place + s + NX) % NX, side, c))
    dev_behind = (rep, tensor_at((place - s + NX) % NX, side, c))

    def y_dev(d):
        return (((y + d) % NY) * NH + h, ten)

    def h_dev(d):
        return (y * NH + (h + d) % NH, ten)

    peers = [sib, far, diag, dev_ahead, dev_behind]
    peers += [y_dev(d) for d in range(1, NY)] + [h_dev(d) for d in range(1, NH)]
    y_order = (4, 3, 5, 2, 6, 1, 7)
    h_order = (2, 1, 3)
    barrier = pltpu.get_barrier_semaphore()
    for dev in peers:
        pl.semaphore_signal(barrier, inc=1, device_id=dev, device_id_type=MESH)

    def remote(src, dst, send, recv, dev):
        return pltpu.make_async_remote_copy(
            src_ref=src, dst_ref=dst, send_sem=send, recv_sem=recv, device_id=dev, device_id_type=MESH
        )

    def part(i, n):
        return pl.ds(pl.multiple_of(i * n, n), n)

    def tokens(qq, first_row, n):
        return pl.ds(pl.multiple_of(qq * TOK + first_row, 16), n)

    def x_cols(g, cc, j):
        ss = 1 - 2 * cc
        shift = (2, ss + NX, NX - ss, 0)[j]
        return part(tensor_at((place + shift) % NX, g, cc), ROWS)

    def local(src, dst, sem):
        copy = pltpu.make_async_copy(src, dst, sem)
        copy.start()
        return copy

    w_copy = local(weight, w32, local_sem.at[0])
    c_copy = local(cot, cq.at[part(q, TOK)], local_sem.at[1])
    x_copies = [local(act.at[:, x_cols(side, c, j)], xq.at[j, part(q, TOK)], local_sem.at[2 + j]) for j in range(4)]
    small_copies = [
        local(anchor, old_anchor, local_sem.at[6]),
        local(mom, old_mom, local_sem.at[7]),
        local(frag, frag_v, local_sem.at[8]),
    ]
    moment_copies = [local(first, f32, local_sem.at[9]), local(second, v32, local_sem.at[10])]

    pl.semaphore_wait(barrier, len(peers))

    sends = []

    def start(copy):
        copy.start()
        sends.append(copy)
        return copy

    targets = ((1, far, others[1]), (2, diag, others[2]), (0, sib, others[0]))

    def x_issue(u):
        j, k = u // UNITS, u % UNITS
        for e, dev, (g, cc) in targets:
            src = act.at[pl.ds(k * CUT, CUT), x_cols(g, cc, j)]
            start(remote(src, xq.at[j, tokens(q, k * CUT, CUT)], x_send.at[u, e], x_recv.at[u, e], dev))

    def x_wait(u):
        j, k = u // UNITS, u % UNITS
        if k == 0:
            x_copies[j].wait()
        for e, qq in enumerate((q_sib, q_far, q_diag)):
            src = act.at[pl.ds(0, CUT), pl.ds(0, ROWS)]
            dst = xq.at[j, tokens(qq, k * CUT, CUT)]
            remote(src, dst, x_send.at[u, e], x_recv.at[u, e], sib).wait_recv()
        if u + AHEAD < 4 * UNITS:
            x_issue(u + AHEAD)

    def x_half(i):
        for u in range(i * UNITS // 2, (i + 1) * UNITS // 2):
            x_wait(u)

    def send_features():
        start(remote(cot, cq.at[part(q, TOK)], c_send.at[1], c_recv.at[1], far))
        start(remote(cot, cq.at[part(q, TOK)], c_send.at[0], c_recv.at[0], sib))
        for u in range(AHEAD):
            x_issue(u)

    stage_r = {}

    def send_columns():
        wt[...] = w32[...].T.astype(BF)
        for d in y_order:
            src = wt.at[part((y + d) % NY, BAND)]
            stage_r[d] = start(remote(src, ybuf.at[d], r_send.at[d], r_recv.at[d], y_dev(d)))

    send_features()
    w_copy.wait()
    wq[3] = w32[...].astype(BF)
    w_ahead = start(remote(wq.at[3], wq.at[2], w_send.at[0], w_recv.at[0], dev_ahead))
    w_behind = start(remote(wq.at[3], wq.at[1], w_send.at[1], w_recv.at[1], dev_behind))
    send_columns()
    for copy in small_copies:
        copy.wait()
    m_res[...] = jnp.broadcast_to((frag_v[...] == 1).astype(F32), (128, ROWS)).T

    w_ahead.wait_recv()
    w_pass = start(remote(wq.at[2], wq.at[0], w_send.at[2], w_recv.at[2], dev_ahead))
    remote(cot, cq.at[part(q_far, TOK)], c_send.at[1], c_recv.at[1], far).wait_recv()
    start(remote(cq.at[part(q_far, TOK)], cq.at[part(q_far, TOK)], c_send.at[2], c_recv.at[2], sib))

    def grad(j):
        return lax.dot_general(xq[j], cq[...], (((0,), (0,)), ((), ())), preferred_element_type=F32)

    def project(j):
        return jnp.dot(xq[j], wq[j], preferred_element_type=F32)

    stage_h = {}

    def sum_y():
        total = wt[part(y, BAND), :].astype(F32)
        for d in y_order:
            stage_r[d].wait_recv()
            total = total + ybuf[d].astype(F32)
        s32[...] = total
        s16[...] = total.astype(BF)
        for d in h_order:
            src = s16.at[part((h + d) % NH, COLS)]
            stage_h[d] = start(remote(src, zbuf.at[d], h_send.at[d], h_recv.at[d], h_dev(d)))

    def outer_step():
        total = s32[part(h, COLS), :]
        for d in h_order:
            stage_h[d].wait_recv()
            total = total + zbuf[d].astype(F32)
        inside = frag_v[...] == 1
        pseudo = old_anchor[...] - total * (1.0 / (NY * NH))
        momentum = OUTER_MU * old_mom[...] + pseudo
        moved = old_anchor[...] - OUTER_RATE * (pseudo + OUTER_MU * momentum)
        own = part(rep, COLS)
        at[own, :] = jnp.where(inside, MIX_SHARE * moved, 0.0).astype(BF)
        for d in h_order:
            start(remote(at.at[own], at.at[own], b_send.at[d], b_recv.at[d], h_dev(d)))
        anchor_out[...] = jnp.where(inside, moved, old_anchor[...])
        mom_out[...] = jnp.where(inside, momentum, old_mom[...])

    def gather_y():
        for d in h_order:
            theirs = part(y * NH + (h - d + NH) % NH, COLS)
            remote(at.at[theirs], at.at[theirs], b_send.at[d], b_recv.at[d], h_dev(d)).wait_recv()
        for d in y_order:
            start(remote(at.at[part(y, BAND)], at.at[part(y, BAND)], a_send.at[d], a_recv.at[d], y_dev(d)))

    def outer(u):
        for place, stage in zip(PLACES, (sum_y, outer_step, gather_y)):
            if place == u:
                stage()

    x_half(0)
    outer(0)
    x_half(1)
    remote(cot, cq.at[part(q_sib, TOK)], c_send.at[0], c_recv.at[0], sib).wait_recv()
    remote(cot, cq.at[part(q_diag, TOK)], c_send.at[2], c_recv.at[2], sib).wait_recv()
    c_copy.wait()
    g_send[0] = grad(0).astype(BF)
    to_opp = start(remote(g_send.at[0], g_opp, gs_send.at[0], gs_recv.at[0], dev_ahead))
    outer(1)

    x_half(2)
    w_pass.wait_recv()
    acc[...] = project(0)
    outer(2)
    x_half(3)
    g = grad(1)
    to_opp.wait_recv()
    g_send[1] = (g + g_opp[...].astype(F32)).astype(BF)
    to_ahead = start(remote(g_send.at[1], g_sum, gs_send.at[1], gs_recv.at[1], dev_ahead))
    outer(3)

    x_half(4)
    w_behind.wait_recv()
    acc[...] += project(1)
    outer(4)
    x_half(5)
    g_send[2] = grad(2).astype(BF)
    to_behind = start(remote(g_send.at[2], g_dir, gs_send.at[2], gs_recv.at[2], dev_behind))
    acc[...] += project(2)
    outer(5)

    def last(qq, r, n):
        rows = tokens(qq, r, n)
        return acc[rows, :] + jnp.dot(xq[3, rows, :], wq[3], preferred_element_type=F32)

    mids, sibs, fars = {}, {}, {}
    for k, (r, n) in enumerate(PARTS):
        here = pl.ds(r, n)
        for u in range(r // CUT, (r + n) // CUT):
            x_wait(3 * UNITS + u)
        ym_out[here, :] = last(q_diag, r, n).astype(BF)
        mids[k] = start(remote(ym_out.at[here], ym_in.at[here], ym_send.at[k], ym_recv.at[k], sib))
        ys_out[here, :] = last(q_sib, r, n).astype(BF)
        sibs[k] = start(remote(ys_out.at[here], ys_in.at[here], ys_send.at[k], ys_recv.at[k], sib))
        beyond = last(q_far, r, n)
        own_rows = tokens(q, r, n)
        acc[own_rows, :] = last(q, r, n)
        mids[k].wait_recv()
        yf_out[here, :] = (beyond + ym_in[here, :].astype(F32)).astype(BF)
        fars[k] = start(remote(yf_out.at[here], yf_in.at[here], yf_send.at[k], yf_recv.at[k], far))
        outer(6 + k)

    g_res[...] = grad(3)
    to_ahead.wait_recv()
    to_behind.wait_recv()
    for copy in moment_copies:
        copy.wait()

    def inner_step(i, carry):
        r = part(i, 32)
        gradient = (g_res[r, :] + g_sum[r, :].astype(F32) + g_dir[r, :].astype(F32)) * SCALE
        moment = FIRST_DECAY * f32[r, :] + (1.0 - FIRST_DECAY) * gradient
        square = SECOND_DECAY * v32[r, :] + (1.0 - SECOND_DECAY) * gradient * gradient
        first_out[r, :] = moment
        second_out[r, :] = square
        first_hat = moment / (1.0 - FIRST_DECAY**STEP)
        second_hat = square / (1.0 - SECOND_DECAY**STEP)
        update = first_hat / (jnp.sqrt(second_hat) + ADAM_EPS) + WEIGHT_DECAY * w32[r, :]
        inner = w32[r, :] - INNER_RATE * update
        share = 1.0 - MIX_SHARE * m_res[r, :][:, :1]
        w32[r, :] = inner * share
        return carry

    lax.fori_loop(0, ROWS // 32, inner_step, 0)

    for k, (r, n) in enumerate(PARTS):
        here = pl.ds(r, n)
        sibs[k].wait_recv()
        fars[k].wait_recv()
        total = acc[tokens(q, r, n), :] + ys_in[here, :].astype(F32) + yf_in[here, :].astype(F32)
        y_out[here, :] = (total * SCALE).astype(BF)

    for d in y_order:
        theirs = part((y - d + NY) % NY, BAND)
        remote(at.at[theirs], at.at[theirs], a_send.at[d], a_recv.at[d], y_dev(d)).wait_recv()
    w_out[...] = w32[...] + at[...].astype(F32).T

    for copy in sends:
        copy.wait_send()


def finish(*refs):
    sources, results, sems = refs[:6], refs[6:12], refs[12]
    copies = [pltpu.make_async_copy(a, b, sems.at[i]) for i, (a, b) in enumerate(zip(sources, results))]
    for copy in copies:
        copy.start()
    for copy in copies:
        copy.wait()


def body(
    activations,
    cotangent,
    weight,
    first_moment,
    second_moment,
    anchor,
    outer_momentum,
    fragment_rows,
):
    hbm = pl.BlockSpec(memory_space=pltpu.HBM)
    held = pl.BlockSpec(memory_space=pltpu.VMEM)
    dma = pltpu.SemaphoreType.DMA
    vm = pltpu.VMEM
    shape = jax.ShapeDtypeStruct
    out_shape = (
        shape((ROWS, C), F32),
        shape((ROWS, C), F32),
        shape((ROWS, C), F32),
        shape((COLS, ROWS), F32),
        shape((COLS, ROWS), F32),
        shape((TOK, C), BF),
    )
    results = pl.pallas_call(
        exchange,
        out_shape=tuple(vm(a.shape, a.dtype) for a in out_shape),
        in_specs=[hbm] * 8,
        out_specs=[held] * 6,
        scratch_shapes=[
            vm((ROWS, C), F32),
            vm((ROWS, C), F32),
            vm((ROWS, C), F32),
            vm((COLS, ROWS), F32),
            vm((COLS, ROWS), F32),
            vm((1, ROWS), jnp.int32),
            vm((4, 4 * TOK, ROWS), BF),
            vm((4 * TOK, C), BF),
            vm((4, ROWS, C), BF),
            vm((4 * TOK, C), F32),
            vm((3, ROWS, C), BF),
            vm((ROWS, C), BF),
            vm((ROWS, C), BF),
            vm((ROWS, C), BF),
            vm((ROWS, C), F32),
            vm((TOK, C), BF),
            vm((TOK, C), BF),
            vm((TOK, C), BF),
            vm((TOK, C), BF),
            vm((TOK, C), BF),
            vm((TOK, C), BF),
            vm((C, ROWS), BF),
            vm((NY, BAND, ROWS), BF),
            vm((BAND, ROWS), F32),
            vm((BAND, ROWS), BF),
            vm((NH, COLS, ROWS), BF),
            vm((C, ROWS), BF),
            vm((ROWS, 128), F32),
            dma((11,)),
            dma((4 * UNITS, 3)),
            dma((4 * UNITS, 3)),
            dma((3,)),
            dma((3,)),
            dma((3,)),
            dma((3,)),
            dma((3,)),
            dma((3,)),
            dma((len(PARTS),)),
            dma((len(PARTS),)),
            dma((len(PARTS),)),
            dma((len(PARTS),)),
            dma((len(PARTS),)),
            dma((len(PARTS),)),
            dma((NY,)),
            dma((NY,)),
            dma((NH,)),
            dma((NH,)),
            dma((NH,)),
            dma((NH,)),
            dma((NY,)),
            dma((NY,)),
        ],
        compiler_params=pltpu.CompilerParams(
            collective_id=0, has_side_effects=True, vmem_limit_bytes=32 * 1024 * 1024
        ),
        name="exchange",
    )(
        *(
            pltpu.with_memory_space_constraint(a, pltpu.HBM)
            for a in (
                activations[0],
                cotangent[0],
                weight[0],
                anchor.T,
                outer_momentum.T,
                fragment_rows[None, :],
                first_moment[0],
                second_moment[0],
            )
        )
    )

    weight_out, first_new, second_new, anchor_new, momentum_new, projected = pl.pallas_call(
        finish,
        out_shape=out_shape,
        in_specs=[held] * 6,
        out_specs=[hbm] * 6,
        scratch_shapes=[dma((6,))],
        compiler_params=pltpu.CompilerParams(vmem_limit_bytes=8 * 1024 * 1024),
        name="finish",
    )(*(pltpu.with_memory_space_constraint(a, pltpu.VMEM) for a in results))
    return (
        weight_out[None],
        first_new[None],
        second_new[None],
        anchor_new.T,
        momentum_new.T,
        projected[None],
    )


def solution(mesh):
    return jax.shard_map(
        body,
        mesh=mesh,
        in_specs=(
            P("replica", "tensor", None),
            P("replica", "tensor", None),
            P("replica", "tensor", None),
            P("replica", "tensor", None),
            P("replica", "tensor", None),
            P("tensor", "replica"),
            P("tensor", "replica"),
            P("tensor"),
        ),
        out_specs=(
            P("replica", "tensor", None),
            P("replica", "tensor", None),
            P("replica", "tensor", None),
            P("tensor", "replica"),
            P("tensor", "replica"),
            P("replica", "tensor", None),
        ),
        check_vma=False,
    )
```

time: 50.1 us -> 45.3 us (0.904)
  Pallas kernels: 49.3 us -> 44.5 us
    pallas_call x2, Pallas kernels: 49.3 us -> 44.5 us  [the longest x1 43.3 us: body(): pl.pallas_call(exchange, out_shape=tuple((vm(a.shape, a.dtype) for a in o...]
where the time goes in v3:
time: 45.3 us; the launch traced here: 45.2 us
  Pallas kernels  44.5 us (98%)
  between operations  0.64 us (1%)
    pallas_call x1, Pallas kernels, body(): pl.pallas_call(exchange, out_shape=tuple((vm(a.shape, a.dtype) for a in o...  43.3 us
    pallas_call x1, Pallas kernels, body(): pl.pallas_call(finish, out_shape=out_shape, in_specs=[held] * 6, out_spec...  1.26 us

profile of v3, /device:TPU:1, one launch (start us, length us, event | category | flops | bytes accessed | tf_op | source)
XLA Modules:
  0.0 45.2 jit_solution(12308201639006136495)
XLA Ops:
  0.6 43.3 %exchange.1 = (f32[256,512]{1,0:T(8,128)S(1)}, f32[256,512]{1,0:T(8,128)S(1)}, f32[256,512]{1,0:T(8,128)S(1)}, f32[16,256]{1,0:T(8,128)S(1)}, f32[16,256]{1,0:T(8,128)S(1)}, /*index=5*/bf16[192,512]{1,0:T(8,128)(2,1)S(1)}) custom-call(bf16[192,4096]{1,0:T(8,128)(2,1)} %bitcast.14, bf16[192,512]{1,0:T(8,128)(2,1)} %bitcast.18, f32[256,512]{1,0:T(8,128)} %bitcast.15, ...), custom_call_target="tpu_custom_call" | custom-call | tf_op jit(solution)/shard_map/exchange/pallas_call | solution.py:403
  43.9 1.3 %finish.1 = (f32[256,512]{1,0:T(8,128)}, f32[256,512]{1,0:T(8,128)}, f32[256,512]{1,0:T(8,128)}, f32[16,256]{1,0:T(8,128)}, f32[16,256]{1,0:T(8,128)}, /*index=5*/bf16[192,512]{1,0:T(8,128)(2,1)}) custom-call(f32[256,512]{1,0:T(8,128)S(1)} %get-tuple-element.18.refs_0_, f32[256,512]{1,0:T(8,128)S(1)} %get-tuple-element.19.refs_1_, ...), custom_call_target="tpu_custom_call" | custom-call | tf_op jit(solution)/shard_map/finish/pallas_call | solution.py:481

commit v4 on v3

--- a/solution.py
+++ b/solution.py
@@ -13,8 +13,6 @@
 NH = 4
 ROWS = 256
 TOK = 192
-CUT = 96
-UNITS = TOK // CUT
 COLS = 16
 BAND = NH * COLS
 SCALE = D ** (-0.5)
@@ -31,7 +29,7 @@
 BF = jnp.bfloat16
 F32 = jnp.float32
 MESH = pl.DeviceIdType.MESH
-AHEAD = 2
+AHEAD = 3
 PLACES = (0, 2, 4)
 PARTS = ((0, 96), (96, 96))
 
@@ -79,6 +77,7 @@
     zbuf,
     at,
     m_res,
+    act_v,
     local_sem,
     x_send,
     x_recv,
@@ -167,6 +166,7 @@
         local(mom, old_mom, local_sem.at[7]),
         local(frag, frag_v, local_sem.at[8]),
     ]
+    v_copy = local(act, act_v, local_sem.at[11])
     moment_copies = [local(first, f32, local_sem.at[9]), local(second, v32, local_sem.at[10])]
 
     pl.semaphore_wait(barrier, len(peers))
@@ -180,26 +180,26 @@
 
     targets = ((1, far, others[1]), (2, diag, others[2]), (0, sib, others[0]))
 
+    def unit(u):
+        return (u // 2, *PARTS[u % 2])
+
     def x_issue(u):
-        j, k = u // UNITS, u % UNITS
+        j, r, n = unit(u)
         for e, dev, (g, cc) in targets:
-            src = act.at[pl.ds(k * CUT, CUT), x_cols(g, cc, j)]
-            start(remote(src, xq.at[j, tokens(q, k * CUT, CUT)], x_send.at[u, e], x_recv.at[u, e], dev))
+            src = (act if u < AHEAD else act_v).at[pl.ds(r, n), x_cols(g, cc, j)]
+            start(remote(src, xq.at[j, tokens(q, r, n)], x_send.at[u, e], x_recv.at[u, e], dev))
 
     def x_wait(u):
-        j, k = u // UNITS, u % UNITS
-        if k == 0:
+        j, r, n = unit(u)
+        if r == 0:
             x_copies[j].wait()
         for e, qq in enumerate((q_sib, q_far, q_diag)):
-            src = act.at[pl.ds(0, CUT), pl.ds(0, ROWS)]
-            dst = xq.at[j, tokens(qq, k * CUT, CUT)]
-            remote(src, dst, x_send.at[u, e], x_recv.at[u, e], sib).wait_recv()
-        if u + AHEAD < 4 * UNITS:
+            src = act.at[pl.ds(0, n), pl.ds(0, ROWS)]
+            remote(src, xq.at[j, tokens(qq, r, n)], x_send.at[u, e], x_recv.at[u, e], sib).wait_recv()
+        if u == 0:
+            v_copy.wait()
+        if u + AHEAD < 8:
             x_issue(u + AHEAD)
-
-    def x_half(i):
-        for u in range(i * UNITS // 2, (i + 1) * UNITS // 2):
-            x_wait(u)
 
     def send_features():
         start(remote(cot, cq.at[part(q, TOK)], c_send.at[1], c_recv.at[1], far))
@@ -277,9 +277,9 @@
             if place == u:
                 stage()
 
-    x_half(0)
+    x_wait(0)
     outer(0)
-    x_half(1)
+    x_wait(1)
     remote(cot, cq.at[part(q_sib, TOK)], c_send.at[0], c_recv.at[0], sib).wait_recv()
     remote(cot, cq.at[part(q_diag, TOK)], c_send.at[2], c_recv.at[2], sib).wait_recv()
     c_copy.wait()
@@ -287,22 +287,22 @@
     to_opp = start(remote(g_send.at[0], g_opp, gs_send.at[0], gs_recv.at[0], dev_ahead))
     outer(1)
 
-    x_half(2)
+    x_wait(2)
     w_pass.wait_recv()
     acc[...] = project(0)
     outer(2)
-    x_half(3)
+    x_wait(3)
     g = grad(1)
     to_opp.wait_recv()
     g_send[1] = (g + g_opp[...].astype(F32)).astype(BF)
     to_ahead = start(remote(g_send.at[1], g_sum, gs_send.at[1], gs_recv.at[1], dev_ahead))
     outer(3)
 
-    x_half(4)
+    x_wait(4)
     w_behind.wait_recv()
     acc[...] += project(1)
     outer(4)
-    x_half(5)
+    x_wait(5)
     g_send[2] = grad(2).astype(BF)
     to_behind = start(remote(g_send.at[2], g_dir, gs_send.at[2], gs_recv.at[2], dev_behind))
     acc[...] += project(2)
@@ -315,8 +315,7 @@
     mids, sibs, fars = {}, {}, {}
     for k, (r, n) in enumerate(PARTS):
         here = pl.ds(r, n)
-        for u in range(r // CUT, (r + n) // CUT):
-            x_wait(3 * UNITS + u)
+        x_wait(6 + k)
         ym_out[here, :] = last(q_diag, r, n).astype(BF)
         mids[k] = start(remote(ym_out.at[here], ym_in.at[here], ym_send.at[k], ym_recv.at[k], sib))
         ys_out[here, :] = last(q_sib, r, n).astype(BF)
@@ -434,9 +433,10 @@
             vm((NH, COLS, ROWS), BF),
             vm((C, ROWS), BF),
             vm((ROWS, 128), F32),
-            dma((11,)),
-            dma((4 * UNITS, 3)),
-            dma((4 * UNITS, 3)),
+            vm((TOK, D), BF),
+            dma((12,)),
+            dma((8, 3)),
+            dma((8, 3)),
             dma((3,)),
             dma((3,)),
             dma((3,)),

time: 45.3 us -> 44.5 us (0.982)
  Pallas kernels: 44.5 us -> 43.7 us
    pallas_call x1, Pallas kernels: 43.3 us -> 42.5 us  [body(): pl.pallas_call(exchange, out_shape=tuple((vm(a.shape, a.dtype) for a in o...]
where the time goes in v4:
time: 44.5 us; the launch traced here: 44.4 us
  Pallas kernels  43.7 us (98%)
  between operations  0.64 us (1%)
    pallas_call x1, Pallas kernels, body(): pl.pallas_call(exchange, out_shape=tuple((vm(a.shape, a.dtype) for a in o...  42.5 us
    pallas_call x1, Pallas kernels, body(): pl.pallas_call(finish, out_shape=out_shape, in_specs=[held] * 6, out_spec...  1.26 us

profile of v4, /device:TPU:1, one launch (start us, length us, event | category | flops | bytes accessed | tf_op | source)
XLA Modules:
  0.0 44.4 jit_solution(12934260337617074560)
XLA Ops:
  0.6 42.5 %exchange.1 = (f32[256,512]{1,0:T(8,128)S(1)}, f32[256,512]{1,0:T(8,128)S(1)}, f32[256,512]{1,0:T(8,128)S(1)}, f32[16,256]{1,0:T(8,128)S(1)}, f32[16,256]{1,0:T(8,128)S(1)}, /*index=5*/bf16[192,512]{1,0:T(8,128)(2,1)S(1)}) custom-call(bf16[192,4096]{1,0:T(8,128)(2,1)} %bitcast.14, bf16[192,512]{1,0:T(8,128)(2,1)} %bitcast.18, f32[256,512]{1,0:T(8,128)} %bitcast.15, ...), custom_call_target="tpu_custom_call" | custom-call | tf_op jit(solution)/shard_map/exchange/pallas_call | solution.py:402
  43.1 1.3 %finish.1 = (f32[256,512]{1,0:T(8,128)}, f32[256,512]{1,0:T(8,128)}, f32[256,512]{1,0:T(8,128)}, f32[16,256]{1,0:T(8,128)}, f32[16,256]{1,0:T(8,128)}, /*index=5*/bf16[192,512]{1,0:T(8,128)(2,1)}) custom-call(f32[256,512]{1,0:T(8,128)S(1)} %get-tuple-element.18.refs_0_, f32[256,512]{1,0:T(8,128)S(1)} %get-tuple-element.19.refs_1_, ...), custom_call_target="tpu_custom_call" | custom-call | tf_op jit(solution)/shard_map/finish/pallas_call | solution.py:481

commit v5 on v4

--- a/solution.py
+++ b/solution.py
@@ -351,6 +351,10 @@
 
     lax.fori_loop(0, ROWS // 32, inner_step, 0)
 
+    last_sums = sends.pop()
+    for copy in sends:
+        copy.wait_send()
+
     for k, (r, n) in enumerate(PARTS):
         here = pl.ds(r, n)
         sibs[k].wait_recv()
@@ -363,8 +367,7 @@
         remote(at.at[theirs], at.at[theirs], a_send.at[d], a_recv.at[d], y_dev(d)).wait_recv()
     w_out[...] = w32[...] + at[...].astype(F32).T
 
-    for copy in sends:
-        copy.wait_send()
+    last_sums.wait_send()
 
 
 def finish(*refs):

time: 44.5 us -> 44.4 us (level)
  no operation moved by 1% of the time
where the time goes in v5:
time: 44.4 us; the launch traced here: 44.3 us
  Pallas kernels  43.7 us (98%)
  between operations  0.64 us (1%)
    pallas_call x1, Pallas kernels, body(): pl.pallas_call(exchange, out_shape=tuple((vm(a.shape, a.dtype) for a in o...  42.4 us
    pallas_call x1, Pallas kernels, body(): pl.pallas_call(finish, out_shape=out_shape, in_specs=[held] * 6, out_spec...  1.26 us

profile of v5, /device:TPU:1, one launch (start us, length us, event | category | flops | bytes accessed | tf_op | source)
XLA Modules:
  0.0 44.3 jit_solution(3599665303550877554)
XLA Ops:
  0.6 42.4 %exchange.1 = (f32[256,512]{1,0:T(8,128)S(1)}, f32[256,512]{1,0:T(8,128)S(1)}, f32[256,512]{1,0:T(8,128)S(1)}, f32[16,256]{1,0:T(8,128)S(1)}, f32[16,256]{1,0:T(8,128)S(1)}, /*index=5*/bf16[192,512]{1,0:T(8,128)(2,1)S(1)}) custom-call(bf16[192,4096]{1,0:T(8,128)(2,1)} %bitcast.14, bf16[192,512]{1,0:T(8,128)(2,1)} %bitcast.18, f32[256,512]{1,0:T(8,128)} %bitcast.15, ...), custom_call_target="tpu_custom_call" | custom-call | tf_op jit(solution)/shard_map/exchange/pallas_call | solution.py:405
  43.0 1.3 %finish.1 = (f32[256,512]{1,0:T(8,128)}, f32[256,512]{1,0:T(8,128)}, f32[256,512]{1,0:T(8,128)}, f32[16,256]{1,0:T(8,128)}, f32[16,256]{1,0:T(8,128)}, /*index=5*/bf16[192,512]{1,0:T(8,128)(2,1)}) custom-call(f32[256,512]{1,0:T(8,128)S(1)} %get-tuple-element.18.refs_0_, f32[256,512]{1,0:T(8,128)S(1)} %get-tuple-element.19.refs_1_, ...), custom_call_target="tpu_custom_call" | custom-call | tf_op jit(solution)/shard_map/finish/pallas_call | solution.py:484
